TPU v7x, 32 devices: a whole 2x2x4 slice. The times are simulated.
32 devices in a mesh: member: 16 (over z, y, core), tensor: 2 (over x).
Axes of the slice: x: 2, y: 2, z: 4, core: 2. Of those that a mesh axis runs over, the one named last changes fastest.
Arguments:
- prompt_states: bfloat16 [8192, 5120], P('member', 'tensor'), may hold values from -6 to 6
- decode_states: bfloat16 [4096, 5120], P('member', 'tensor'), may hold values from -6 to 6
- norm_gain: bfloat16 [5120], P('tensor'), may hold values from 0.5 to 7, as said below
- query_bias: bfloat16 [5120], P('tensor'), may hold values from -3 to 3
- value_bias: bfloat16 [1024], P('tensor'), may hold values from -3 to 3
- w_query: bfloat16 [5120, 5120], P('member', 'tensor'), may hold values from -0.078125 to 0.078125
- w_key: bfloat16 [5120, 1024], P('member', 'tensor'), may hold values from -0.078125 to 0.078125
- w_value: bfloat16 [5120, 1024], P('member', 'tensor'), may hold values from -0.078125 to 0.078125
- w_out: bfloat16 [5120, 5120], P('tensor', 'member'), may hold values from -0.078125 to 0.078125
- targets: bfloat16 [4096, 5120], P('member', 'tensor'), may hold values from -3 to 3
- lengths: int32 [32], replicated, may hold values from 1 to 128, 2048 in all
- seeds: int32 [16], replicated, may hold values from 0 to 46336
Outputs:
- fitness: float32 [32], replicated
- grad_query: float32 [5120, 5120], P('member', 'tensor')
- grad_key: float32 [5120, 1024], P('member', 'tensor')
- grad_value: float32 [5120, 1024], P('member', 'tensor')
- grad_out: float32 [5120, 5120], P('tensor', 'member')
Inputs may be any that keep to these rules, and one draw needn't show every extreme that they name: lengths[2 m] and lengths[2 m + 1] belong to pair m; all lengths sum to exactly 2048, and one of them equals 128. `norm_gain`: positive gains.
All inputs are finite; a program needn't handle non-finite values.
Results may differ from a plain program's by a relative error of at most 0.018.
The roundings to bfloat16 on the way count: a program that leaves them out, or rounds other values in their place, can miss the bound.
Values may be sent and summed in bfloat16 or wider, within the bound.
A program may use at most 192 MiB of HBM per device.

v0:
```python
import math

import jax
import jax.numpy as jnp
from jax import lax
from jax.sharding import PartitionSpec as P

D = 5120
HEADS = 40
KV_HEADS = 8
HEAD_DIM = 128
DEC = 128
RANK = 16


PRIME = 46337
SIGMA_SCALE = 0.3
NEG_LARGE = -1e30


def noise_table(seed_value, matrix_id, positions, rank_count):
    rank_ids = jnp.arange(rank_count, dtype=jnp.int32)
    mixing_matrix = (
        seed_value + (matrix_id * rank_count + rank_ids)[None, :] * 2749 + positions[:, None] * 6271
    ) % PRIME
    hashed = (mixing_matrix * mixing_matrix + 1013) % PRIME
    hashed = (hashed * hashed + mixing_matrix) % PRIME
    hashed = (hashed * hashed + 1013) % PRIME
    return ((hashed.astype(jnp.float32) * (2.0 / PRIME) - 1.0) * math.sqrt(3.0)).astype(
        jnp.bfloat16
    )


def normed(states, gain):
    values = states.astype(jnp.float32)
    scale = lax.rsqrt(jnp.mean(values * values, axis=-1, keepdims=True) + 1e-06)
    return (values * scale * gain.astype(jnp.float32)).astype(jnp.bfloat16)


def expand(inner, table_b):
    return jnp.dot(inner, table_b.astype(jnp.float32).T, precision=lax.Precision.HIGHEST)


def attend(query, keys, values, group, head_dim, prompt_len):
    count = query.shape[0]
    kv_count = keys.shape[1] // head_dim
    query_four = query.reshape(count, kv_count, group, head_dim)
    keys_three = keys.reshape(-1, kv_count, head_dim)
    values_three = values.reshape(-1, kv_count, head_dim)
    scores = jnp.einsum(
        "pkgd,nkd->kgpn", query_four, keys_three, preferred_element_type=jnp.float32
    ) / math.sqrt(head_dim)
    key_index = jnp.arange(keys_three.shape[0], dtype=jnp.int32) - prompt_len
    query_index = jnp.arange(count, dtype=jnp.int32)
    allowed = key_index[None, :] <= query_index[:, None]
    scores = jnp.where(allowed, scores, NEG_LARGE)
    top = jnp.max(scores, axis=-1, keepdims=True)
    exponent = jnp.exp(scores - top)
    weights = (exponent / jnp.sum(exponent, axis=-1, keepdims=True)).astype(jnp.bfloat16)
    mixed = jnp.einsum("kgpn,nkd->pkgd", weights, values_three, preferred_element_type=jnp.float32)
    return mixed.astype(jnp.bfloat16).reshape(count, kv_count * group * head_dim)


def per_device(
    prompt_states,
    decode_states,
    norm_gain,
    query_bias,
    value_bias,
    w_query,
    w_key,
    w_value,
    w_out,
    targets,
    lengths,
    seeds,
):
    members = lax.axis_size("member")
    member_id = lax.axis_index("member")
    tensor_id = lax.axis_index("tensor")
    shard_width = prompt_states.shape[1]
    prompt_len = prompt_states.shape[0]
    query_width = w_query.shape[1]
    pair_width = w_key.shape[1]
    piece_rows = w_query.shape[0]
    out_piece = w_out.shape[1]
    group = HEADS // KV_HEADS
    sigma = SIGMA_SCALE / math.sqrt(D)
    lift = sigma / math.sqrt(RANK)
    seed_value = seeds[member_id]
    length_plus = lengths[2 * member_id]
    negative_length = lengths[2 * member_id + 1]
    local_rows = jnp.arange(2 * DEC, dtype=jnp.int32)
    plus_rows = local_rows < DEC
    positions = local_rows % DEC
    row_live = positions < jnp.where(plus_rows, length_plus, negative_length)
    column_signs = jnp.where(plus_rows, 1.0, -1.0).astype(jnp.float32)[:, None]
    prompt_full, decode_full, gain_full = (
        lax.all_gather(prompt_states, "tensor", axis=1, tiled=True),
        lax.all_gather(decode_states, "tensor", axis=1, tiled=True),
        lax.all_gather(norm_gain[None, :], "tensor", axis=1, tiled=True),
    )
    gain_row = gain_full[0]
    prompt_normed = normed(prompt_full, gain_row)
    decode_normed = normed(decode_full, gain_row)
    pieces = (
        lax.all_gather(w_query, "member", axis=0, tiled=True),
        lax.all_gather(w_key, "member", axis=0, tiled=True),
        lax.all_gather(w_value, "member", axis=0, tiled=True),
    )
    query_base = jnp.dot(decode_normed, pieces[0], preferred_element_type=jnp.float32)
    key_base = jnp.dot(decode_normed, pieces[1], preferred_element_type=jnp.float32)
    value_base = jnp.dot(decode_normed, pieces[2], preferred_element_type=jnp.float32)
    prompt_key_base = jnp.dot(prompt_normed, pieces[1], preferred_element_type=jnp.float32)
    prompt_value_base = jnp.dot(prompt_normed, pieces[2], preferred_element_type=jnp.float32)
    row_ids = jnp.arange(D, dtype=jnp.int32)
    query_cols = tensor_id * query_width + jnp.arange(query_width, dtype=jnp.int32)
    pair_cols = tensor_id * pair_width + jnp.arange(pair_width, dtype=jnp.int32)
    tables_left = jnp.concatenate(
        [
            noise_table(seed_value, 0, row_ids, RANK),
            noise_table(seed_value, 1, row_ids, RANK),
            noise_table(seed_value, 2, row_ids, RANK),
        ],
        axis=1,
    )
    decode_inner = jnp.dot(decode_normed, tables_left, preferred_element_type=jnp.float32)
    prompt_inner = jnp.dot(prompt_normed, tables_left[:, RANK:], preferred_element_type=jnp.float32)
    table_key = noise_table(seed_value, 5, pair_cols, RANK)
    table_value = noise_table(seed_value, 6, pair_cols, RANK)
    low_query = expand(decode_inner[:, :RANK], noise_table(seed_value, 4, query_cols, RANK))
    low_key = expand(decode_inner[:, RANK : 2 * RANK], table_key)
    low_value = expand(decode_inner[:, 2 * RANK :], table_value)
    low_prompt_key = expand(prompt_inner[:, :RANK], table_key)
    low_prompt_value = expand(prompt_inner[:, RANK:], table_value)
    query = (query_base + query_bias.astype(jnp.float32) + column_signs * lift * low_query).astype(
        jnp.bfloat16
    )
    key = (key_base + column_signs * lift * low_key).astype(jnp.bfloat16)
    value = (value_base + value_bias.astype(jnp.float32) + column_signs * lift * low_value).astype(
        jnp.bfloat16
    )
    mixed_parts = []
    for sign_index in range(2):
        sign = 1.0 - 2.0 * sign_index
        first = sign_index * DEC
        last = first + DEC
        prompt_key = (prompt_key_base + sign * lift * low_prompt_key).astype(jnp.bfloat16)
        prompt_value = (
            prompt_value_base + value_bias.astype(jnp.float32) + sign * lift * low_prompt_value
        ).astype(jnp.bfloat16)
        mixed_parts.append(
            attend(
                query[first:last],
                jnp.concatenate([prompt_key, key[first:last]], axis=0),
                jnp.concatenate([prompt_value, value[first:last]], axis=0),
                group,
                HEAD_DIM,
                prompt_len,
            )
        )
    mixed = jnp.concatenate(mixed_parts, axis=0)
    out_base = jnp.dot(
        mixed,
        lax.all_gather(w_out, "member", axis=1, tiled=True),
        preferred_element_type=jnp.float32,
    )
    out_inner = jnp.dot(
        mixed, noise_table(seed_value, 3, query_cols, RANK), preferred_element_type=jnp.float32
    )
    out_low = expand(out_inner, noise_table(seed_value, 7, row_ids, RANK))
    partial_out = (out_base + column_signs * lift * out_low).astype(jnp.bfloat16)
    summed = lax.psum(partial_out, "tensor").astype(jnp.float32)
    shared = lax.dynamic_slice_in_dim(summed, tensor_id * shard_width, shard_width, 1)
    difference = shared - targets.astype(jnp.float32)
    fitness_errors = jnp.sum(difference * difference, axis=1) / D
    fitness_errors = jnp.where(row_live, fitness_errors, 0.0)
    pair_total = lax.psum(
        jnp.stack(
            [
                jnp.sum(fitness_errors[:DEC]) / length_plus.astype(jnp.float32),
                jnp.sum(fitness_errors[DEC:]) / negative_length.astype(jnp.float32),
            ]
        ),
        "tensor",
    )
    fitness = -lax.all_gather(pair_total, "member", axis=0, tiled=True)
    differences = fitness[0::2] - fitness[1::2]
    factor = 1.0 / (2.0 * members * sigma * math.sqrt(RANK))
    row_of_weights = differences * factor
    own_rows = member_id * piece_rows + jnp.arange(piece_rows, dtype=jnp.int32)
    own_out_cols = member_id * out_piece + jnp.arange(out_piece, dtype=jnp.int32)

    def update(first_id, second_id, left_ids, right_ids):
        left_factor = jax.vmap(lambda seed_one: noise_table(seed_one, first_id, left_ids, RANK))(
            seeds
        ).astype(jnp.float32)
        right_factor = jax.vmap(lambda seed_one: noise_table(seed_one, second_id, right_ids, RANK))(
            seeds
        ).astype(jnp.float32)
        return jnp.einsum(
            "lqh,lah->qa",
            left_factor * row_of_weights[:, None, None],
            right_factor,
            precision=lax.Precision.HIGHEST,
        )

    grad_query = update(0, 4, own_rows, query_cols)
    grad_key = update(1, 5, own_rows, pair_cols)
    grad_value = update(2, 6, own_rows, pair_cols)
    grad_out = update(3, 7, query_cols, own_out_cols)
    return (fitness, grad_query, grad_key, grad_value, grad_out)


def solution(mesh):
    placed = (
        P("member", "tensor"),
        P("member", "tensor"),
        P("tensor"),
        P("tensor"),
        P("tensor"),
        P("member", "tensor"),
        P("member", "tensor"),
        P("member", "tensor"),
        P("tensor", "member"),
        P("member", "tensor"),
        P(),
        P(),
    )
    return jax.shard_map(
        per_device,
        mesh=mesh,
        in_specs=placed,
        out_specs=(
            P(),
            P("member", "tensor"),
            P("member", "tensor"),
            P("member", "tensor"),
            P("tensor", "member"),
        ),
        check_vma=False,
    )
```

profile of v0, /device:TPU:0, one launch (start us, length us, event | category | flops | bytes accessed | tf_op | source)
XLA Modules:
  0.0 683.0 jit_solution(12345693242278420061)
XLA Ops:
  11.2 5.3 all-gather.1
  26.1 25.2 %all-gather.13.cloned.1.call-done = bf16[256,5120]{1,0:T(8,128)(2,1)} async-done(((bf16[256,2560]{1,0:T(8,128)(2,1)}), bf16[256,5120]{1,0:T(8,128)(2,1)}) %all-gather.13.cloned.1.call-update) | async-done | bytes 2621456 | tf_op jit(solution)/shard_map/all_gather | solution.py:100
  54.8 66.7 %all-gather.9.cloned.1.call-done = bf16[512,5120]{1,0:T(8,128)(2,1)} async-done(((bf16[512,2560]{1,0:T(8,128)(2,1)}), bf16[512,5120]{1,0:T(8,128)(2,1)}) %all-gather.9.cloned.1.call-update) | async-done | bytes 5242896 | tf_op jit(solution)/shard_map/all_gather | solution.py:99
  121.5 3.7 fusion.2
  131.9 47.8 %all-gather.15.cloned.1.call-done = bf16[5120,512]{1,0:T(8,128)(2,1)} async-done(((bf16[320,512]{1,0:T(8,128)(2,1)}), bf16[5120,512]{1,0:T(8,128)(2,1)}) %all-gather.15.cloned.1.call-update) | async-done | bytes 5242896 | tf_op jit(solution)/shard_map/all_gather | solution.py:108
  179.8 4.2 fusion.517
  185.2 6.4 add_convert_fusion.2
  194.4 42.1 %all-gather.11.cloned.1.call-done = bf16[5120,512]{1,0:T(8,128)(2,1)} async-done(((bf16[320,512]{1,0:T(8,128)(2,1)}), bf16[5120,512]{1,0:T(8,128)(2,1)}) %all-gather.11.cloned.1.call-update) | async-done | bytes 5242896 | tf_op jit(solution)/shard_map/all_gather | solution.py:109
  236.5 4.2 convolution_add_fusion.2
  242.8 6.1 add_convert_fusion.3
  251.4 118.7 %all-gather.17.cloned.1.call-done = bf16[5120,2560]{1,0:T(8,128)(2,1)} async-done(((bf16[320,2560]{1,0:T(8,128)(2,1)}), bf16[5120,2560]{1,0:T(8,128)(2,1)}) %all-gather.17.cloned.1.call-update) | async-done | bytes 26214416 | tf_op jit(solution)/shard_map/all_gather | solution.py:107
  370.1 14.3 %convolution_add_fusion = f32[256,2560]{1,0:T(8,128)S(1)} fusion(bf16[5120,2560]{1,0:T(8,128)(2,1)} %all-gather.17.cloned.1.call-done, f32[2560]{0:T(1024)S(1)} %convert_element_type.214, bf16[256,5120]{1,0:T(8,128)(2,1)} %all-gather.13.cloned.1.call-done, f32[5120]{0:T(1024)S(1)} %bitcast.80, f32[256]{0:T(256)S(1)} %copy-done.21), kind=kOutput, calls=%fused_computation.27 | convolution fusion | flops 6716784640 | bytes 31489024 | tf_op jit(solution)/shard_map/dot_general | solution.py:111
  389.6 4.7 fusion.526
  397.3 4.0 fusion.59
  402.8 102.3 %all-gather.19.cloned.1.call-done = bf16[2560,5120]{0,1:T(8,128)(2,1)} async-done(((bf16[2560,320]{0,1:T(8,128)(2,1)}), bf16[2560,5120]{0,1:T(8,128)(2,1)}) %all-gather.19.cloned.1.call-update) | async-done | bytes 26214416 | tf_op jit(solution)/shard_map/all_gather | solution.py:165
  505.1 14.6 %fusion.84 = f32[256,5120]{1,0:T(8,128)} fusion(bf16[2560,5120]{0,1:T(8,128)(2,1)} %all-gather.19.cloned.1.call-done, bf16[128,2560]{0,1:T(8,128)(2,1)S(1)} %bitcast.84, bf16[128,2560]{0,1:T(8,128)(2,1)S(1)} %bitcast.82), kind=kOutput, calls=%fused_computation.121 | convolution fusion | flops 6713507840 | bytes 32768000 | tf_op jit(solution)/shard_map/dot_general | solution.py:163
  519.7 6.9 %fusion.6 = bf16[256,5120]{1,0:T(8,128)(2,1)} fusion(f32[256,5120]{1,0:T(8,128)} %fusion.84, f32[256,16]{0,1:T(8,128)S(1)} %fusion.83, f32[256]{0:T(256)S(1)} %copy-done.11, s32[16]{0:T(128)S(1)} %copy-done.24, s32[5120]{0:T(1024)S(1)} %iota_multiply_fusion), kind=kOutput, calls=%fused_computation.17 | convolution fusion | flops 258539520 | bytes 7902272 | tf_op jit(solution)/shard_map/dot_general | solution.py:41
  530.0 71.2 %all-reduce.3.cloned.1.call-done = bf16[256,5120]{1,0:T(8,128)(2,1)} async-done(((bf16[256,5120]{1,0:T(8,128)(2,1)}), bf16[256,5120]{1,0:T(8,128)(2,1)}) %all-reduce.3.cloned.1.call-update) | async-done | bytes 2621456 | tf_op jit(solution)/shard_map/psum | solution.py:173
  607.0 4.9 psum.15
  612.1 32.2 %all-reduce = f32[32]{0:T(128)S(1)} all-reduce(f32[32]{0:T(128)S(1)} %dynamic-update-slice), channel_id=1, replica_groups=mesh['member'=16,'tensor'=2] {'member'}, use_global_device_ids=true, to_apply=%add | all-reduce | flops 32 | bytes 256
  644.5 11.7 %convolution_bitcast_fusion = f32[2560,320]{0,1:T(8,128)} fusion(f32[16]{0:T(128)S(1)} %subtract_multiply_fusion, s32[16,16]{0,1:T(8,128)S(1)} %get-tuple-element.26, s32[2560]{0:T(1024)S(1)} %add_multiply_fusion, s32[16,16]{0,1:T(8,128)S(1)} %get-tuple-element.20, s32[320]{0:T(512)S(1)} %add_multiply_fusion.1), kind=kOutput, calls=%fused_computation.23 | convolution fusion | flops 2544435200 | bytes 3290432 | tf_op jit(solution)/shard_map/lqh,lah->qa/dot_general | solution.py:201
  656.2 11.4 %convolution_bitcast_fusion.1 = f32[320,2560]{1,0:T(8,128)} fusion(s32[2560]{0:T(1024)S(1)} %add_multiply_fusion, s32[16,16]{0,1:T(8,128)S(1)} %get-tuple-element.21, f32[16]{0:T(128)S(1)} %subtract_multiply_fusion, s32[320]{0:T(512)S(1)} %add_multiply_fusion.1, s32[16,16]{0,1:T(8,128)S(1)} %get-tuple-element.27), kind=kOutput, calls=%fused_computation.24 | convolution fusion | flops 2543288320 | bytes 3290432 | tf_op jit(solution)/shard_map/lqh,lah->qa/dot_general | solution.py:201
  667.6 3.9 convolution_bitcast_fusion.2
  671.5 4.2 convolution_bitcast_fusion.3
  (148 shorter events, 47.7 us)
Async XLA Ops:
  7.2 44.1 %all-gather.13.cloned.1.call-start = ((), (), s32[]{:S(2)}) async-start(), calls=%async_computation.2 | async-start | bytes 3932160 | tf_op jit(solution)/shard_map/all_gather | solution.py:100
  7.9 113.6 %all-gather.9.cloned.1.call-start = ((), (), s32[]{:S(2)}) async-start(), calls=%async_computation | async-start | bytes 7864320 | tf_op jit(solution)/shard_map/all_gather | solution.py:99
  8.7 7.9 %copy-start.7 = (bf16[2560]{0:T(1024)(128)(2,1)S(1)}, bf16[2560]{0:T(1024)(128)(2,1)}, u32[]{:S(2)}) copy-start(bf16[2560]{0:T(1024)(128)(2,1)} %param.15) | copy-start | bytes 15364
  8.7 7.9 %copy-start.19 = (bf16[512]{0:T(512)(128)(2,1)S(1)}, bf16[512]{0:T(512)(128)(2,1)}, u32[]{:S(2)}) copy-start(bf16[512]{0:T(512)(128)(2,1)} %param.16) | copy-start | bytes 3076
  8.7 8.5 %copy-start.22 = (s32[16]{0:T(128)S(1)}, s32[16]{0:T(128)}, u32[]{:S(2)}) copy-start(s32[16]{0:T(128)} %param.23) | copy-start | bytes 196
  8.7 171.1 %all-gather.15.cloned.1.call-start = ((), (), s32[]{:S(2)}) async-start(), calls=%async_computation.3 | async-start | bytes 5570560 | tf_op jit(solution)/shard_map/all_gather | solution.py:108
  9.4 227.1 %all-gather.11.cloned.1.call-start = ((), (), s32[]{:S(2)}) async-start(), calls=%async_computation.1 | async-start | bytes 5570560 | tf_op jit(solution)/shard_map/all_gather | solution.py:109
  10.0 360.1 %all-gather.17.cloned.1.call-start = ((), (), s32[]{:S(2)}) async-start(), calls=%async_computation.4 | async-start | bytes 27852800 | tf_op jit(solution)/shard_map/all_gather | solution.py:107
  10.6 494.5 %all-gather.19.cloned.1.call-start = ((), (), s32[]{:S(2)}) async-start(), calls=%async_computation.5 | async-start | bytes 27852800 | tf_op jit(solution)/shard_map/all_gather | solution.py:165
  11.2 590.0 %all-reduce.3.cloned.1.call-start = ((), (), s32[]{:S(2)}) async-start(), calls=%async_computation.6 | async-start | bytes 5242880 | tf_op jit(solution)/shard_map/psum | solution.py:173
  21.0 108.6 %copy-start.30 = (s32[16]{0:T(128)}, s32[16]{0:T(128)S(1)}, u32[]{:S(2)}) copy-start(s32[16]{0:T(128)S(1)} %broadcast_add_fusion.13) | copy-start | bytes 196
  21.7 162.3 %copy-start.9 = (f32[256]{0:T(256)}, f32[256]{0:T(256)S(1)}, u32[]{:S(2)}) copy-start(f32[256]{0:T(256)S(1)} %select_multiply_fusion) | copy-start | bytes 3076
  22.8 161.2 %copy-start.13 = (s32[512]{0:T(512)}, s32[512]{0:T(512)S(1)}, u32[]{:S(2)}) copy-start(s32[512]{0:T(512)S(1)} %add_multiply_fusion.2) | copy-start | bytes 6148
  53.8 126.0 %copy-start.20 = (f32[256]{0:T(256)}, f32[256]{0:T(256)S(1)}, u32[]{:S(2)}) copy-start(f32[256]{0:T(256)S(1)} %add_rsqrt_fusion.1) | copy-start | bytes 3076
  54.8 129.2 %copy-start.8 = (f32[256,48]{0,1:T(8,128)}, f32[256,48]{0,1:T(8,128)S(1)}, u32[]{:S(2)}) copy-start(f32[256,48]{0,1:T(8,128)S(1)} %fusion.123) | copy-start | bytes 147460
  125.5 59.7 %copy-start.17 = (f32[512]{0:T(512)}, f32[512]{0:T(512)S(1)}, u32[]{:S(2)}) copy-start(f32[512]{0:T(512)S(1)} %add_rsqrt_fusion) | copy-start | bytes 6148
  236.5 6.3 copy-start.26
  250.0 120.1 %copy-start.21 = (f32[256]{0:T(256)S(1)}, f32[256]{0:T(256)}, u32[]{:S(2)}) copy-start(f32[256]{0:T(256)} %copy-done.20) | copy-start | bytes 3076
  251.4 133.1 %copy-start.11 = (f32[256]{0:T(256)S(1)}, f32[256]{0:T(256)}, u32[]{:S(2)}) copy-start(f32[256]{0:T(256)} %copy-done.9) | copy-start | bytes 3076
  251.4 133.1 %copy-start.25 = (s32[16]{0:T(128)S(1)}, s32[16]{0:T(128)}, u32[]{:S(2)}) copy-start(s32[16]{0:T(128)} %broadcast_add_fusion.10) | copy-start | bytes 196
  402.8 116.9 %copy-start.24 = (s32[16]{0:T(128)S(1)}, s32[16]{0:T(128)}, u32[]{:S(2)}) copy-start(s32[16]{0:T(128)} %get-tuple-element.34) | copy-start | bytes 196
  526.7 74.5 %copy-start.2 = (bf16[256,2560]{1,0:T(8,128)(2,1)S(1)}, bf16[256,2560]{1,0:T(8,128)(2,1)}, u32[]{:S(2)}) copy-start(bf16[256,2560]{1,0:T(8,128)(2,1)} %param.21) | copy-start | bytes 3932164
  644.3 11.9 %copy-start.32 = (f32[32]{0:T(128)}, f32[32]{0:T(128)S(1)}, u32[]{:S(2)}) copy-start(f32[32]{0:T(128)S(1)} %neg.3) | copy-start | bytes 388
  656.2 11.4 %copy-start.15 = (s32[512]{0:T(512)S(1)}, s32[512]{0:T(512)}, u32[]{:S(2)}) copy-start(s32[512]{0:T(512)} %copy-done.13) | copy-start | bytes 6148
  (18 other events, 49.9 us)
Sparse Core Ops, SparseCore 0:
  9.5 41.7 all-gather.12
  52.8 68.5 all-gather.8
  123.8 55.9 all-gather.14
  181.9 54.5 all-gather.10
  238.0 132.0 all-gather.16
  371.6 133.5 all-gather.18
  526.8 74.3 all-reduce.2
where the time goes:
time: 686 us; the launch traced here: 683 us
  waiting for transfers between devices  478 us (70%)
  matrix products  108 us (16%)
  blocking collectives  42.4 us (6%)
  other arithmetic  27.7 us (4%)
  between operations  18.5 us (3%)
  local copies, waits for them, and re-layouts  8.2 us (1%)
    all_gather x1, waiting for transfers between devices, per_device(): lax.all_gather(w_query, 'member', axis=0, tiled=True)  119 us
    all_gather x1, waiting for transfers between devices, per_device(): lax.all_gather(w_out, 'member', axis=1, tiled=True)  102 us
    psum x1, waiting for transfers between devices, per_device(): summed = lax.psum(partial_out, 'tensor').astype(jnp.float32)  71.2 us
    all_gather x1, waiting for transfers between devices, per_device(): lax.all_gather(prompt_states, 'tensor', axis=1, tiled=True)  66.7 us
    all_gather x1, waiting for transfers between devices, per_device(): lax.all_gather(w_key, 'member', axis=0, tiled=True)  47.8 us
    all_gather x1, waiting for transfers between devices, per_device(): lax.all_gather(w_value, 'member', axis=0, tiled=True)  42.1 us
    unnamed x1, blocking collectives  32.2 us
    dot_general x4, matrix products, update(): jnp.einsum('lqh,lah->qa', left_factor * row_of_weights[:, None, None], ri...  31.1 us
  transfers between devices with their start and end apart: 7, of which 7 were waited for; matrix products, arithmetic and copies ran while one was open for 13% of the time, Pallas kernels for 0%

commit v1 on v0

v1 whole, which is shorter than its diff:
```python
import math

import jax
import jax.numpy as jnp
from jax import lax
from jax.sharding import PartitionSpec as P

D = 5120
HEADS = 40
KV_HEADS = 8
HEAD_DIM = 128
DEC = 128
RANK = 16


PRIME = 46337
SIGMA_SCALE = 0.3
NEG_LARGE = -1e30


def noise_rows(seed_value, matrix_id, positions):
    rank_ids = jnp.arange(RANK, dtype=jnp.int32)
    mixing = (
        seed_value + (matrix_id * RANK + rank_ids)[:, None] * 2749 + positions[None, :] * 6271
    ) % PRIME
    hashed = (mixing * mixing + 1013) % PRIME
    hashed = (hashed * hashed + mixing) % PRIME
    hashed = (hashed * hashed + 1013) % PRIME
    return ((hashed.astype(jnp.float32) * (2.0 / PRIME) - 1.0) * math.sqrt(3.0)).astype(
        jnp.bfloat16
    )


def normed(states, gain):
    values = states.astype(jnp.float32)
    scale = lax.rsqrt(jnp.mean(values * values, axis=-1, keepdims=True) + 1e-06)
    return (values * scale * gain.astype(jnp.float32)).astype(jnp.bfloat16)


def parts_of(values, count):
    parts = []
    for _ in range(count):
        part = lax.reduce_precision(values, 8, 7)
        parts.append(part.astype(jnp.bfloat16))
        values = values - part
    return parts


def expand(inner, rows_b):
    parts = parts_of(inner, 3)
    return jnp.dot(
        jnp.concatenate(parts, axis=1),
        jnp.concatenate([rows_b] * 3, axis=0),
        preferred_element_type=jnp.float32,
    )


def times_rows(left, rows):
    return lax.dot_general(
        left, rows, (((1,), (1,)), ((), ())), preferred_element_type=jnp.float32
    )


def attend(query, keys, values, group, head_dim, prompt_len):
    count = query.shape[0]
    kv_count = keys.shape[1] // head_dim
    query_four = query.reshape(count, kv_count, group, head_dim)
    keys_three = keys.reshape(-1, kv_count, head_dim)
    values_three = values.reshape(-1, kv_count, head_dim)
    scores = jnp.einsum(
        "pkgd,nkd->kgpn", query_four, keys_three, preferred_element_type=jnp.float32
    ) / math.sqrt(head_dim)
    key_index = jnp.arange(keys_three.shape[0], dtype=jnp.int32) - prompt_len
    query_index = jnp.arange(count, dtype=jnp.int32)
    allowed = key_index[None, :] <= query_index[:, None]
    scores = jnp.where(allowed, scores, NEG_LARGE)
    top = jnp.max(scores, axis=-1, keepdims=True)
    exponent = jnp.exp(scores - top)
    weights = (exponent / jnp.sum(exponent, axis=-1, keepdims=True)).astype(jnp.bfloat16)
    mixed = jnp.einsum("kgpn,nkd->pkgd", weights, values_three, preferred_element_type=jnp.float32)
    return mixed.astype(jnp.bfloat16).reshape(count, kv_count * group * head_dim)


def chip_cycle(chips):
    wide = chips // 4
    walk = [(a, 0) for a in range(4)]
    for a in (3, 2, 1, 0):
        columns = list(range(1, wide))
        if a % 2 == 0:
            columns = columns[::-1]
        walk += [(a, b) for b in columns]
    return [a * wide + b for a, b in walk]


def ring_step(piece, cycle, shift):
    count = len(cycle)
    perm = []
    for place, chip in enumerate(cycle):
        other = cycle[(place + shift) % count]
        perm += [(2 * chip + core, 2 * other + core) for core in range(2)]
    return lax.ppermute(piece, "member", perm)


def to_sibling(piece, members):
    return lax.ppermute(piece, "member", [(m, m ^ 1) for m in range(members)])


def ring_gather(shard, cycle, place, after=None):
    count = len(cycle)
    table = jnp.array(cycle, jnp.int32)
    rows = shard.shape[0]
    half = rows // 2
    if after is not None:
        shard, _ = lax.optimization_barrier((shard, after))
    found = [(table[place], shard)]
    forward = backward = shard
    for step in range(1, count // 2):
        forward = ring_step(forward, cycle, 1)
        backward = ring_step(backward, cycle, -1)
        found.append((table[(place - step) % count], forward))
        found.append((table[(place + step) % count], backward))
    forward = ring_step(forward[:half], cycle, 1)
    backward = ring_step(backward[half:], cycle, -1)
    far = table[(place + count // 2) % count]
    found.append((far, jnp.concatenate([forward, backward], axis=0)))
    return found, (forward, backward)


def per_device(
    prompt_states,
    decode_states,
    norm_gain,
    query_bias,
    value_bias,
    w_query,
    w_key,
    w_value,
    w_out,
    targets,
    lengths,
    seeds,
):
    members = lax.axis_size("member")
    tensors = lax.axis_size("tensor")
    member_id = lax.axis_index("member")
    tensor_id = lax.axis_index("tensor")
    core = member_id % 2
    cycle = chip_cycle(members // 2)
    places = [0] * len(cycle)
    for place_at, chip in enumerate(cycle):
        places[chip] = place_at
    place = jnp.array(places, jnp.int32)[member_id // 2]
    shard_width = prompt_states.shape[1]
    prompt_len = prompt_states.shape[0]
    query_width = w_query.shape[1]
    pair_width = w_key.shape[1]
    piece_rows = w_query.shape[0]
    out_piece = w_out.shape[1]
    group = HEADS // KV_HEADS
    sigma = SIGMA_SCALE / math.sqrt(D)
    lift = sigma / math.sqrt(RANK)
    seed_value = seeds[member_id]
    length_plus = lengths[2 * member_id]
    negative_length = lengths[2 * member_id + 1]
    local_rows = jnp.arange(2 * DEC, dtype=jnp.int32)
    plus_rows = local_rows < DEC
    positions = local_rows % DEC
    row_live = positions < jnp.where(plus_rows, length_plus, negative_length)
    column_signs = jnp.where(plus_rows, 1.0, -1.0).astype(jnp.float32)[:, None]

    in_shard = jnp.concatenate([w_query, w_key, w_value], axis=1)
    out_shard = w_out.T
    lane_rows = piece_rows // 2
    query_all = jnp.zeros((D, query_width), jnp.bfloat16)
    pair_all = jnp.zeros((D, 2 * pair_width), jnp.bfloat16)
    out_lanes = []
    for lane in range(2):
        first = lane * lane_rows
        found, last = ring_gather(in_shard[first : first + lane_rows], cycle, place)
        for chip, piece in found:
            for owner, block in ((core, piece), (1 - core, to_sibling(piece, members))):
                start = (2 * chip + owner) * piece_rows + first
                query_all = lax.dynamic_update_slice_in_dim(
                    query_all, block[:, :query_width], start, 0
                )
                pair_all = lax.dynamic_update_slice_in_dim(
                    pair_all, block[:, query_width:], start, 0
                )
        out_found, _ = ring_gather(out_shard[first : first + lane_rows], cycle, place, last)
        out_lanes.append(out_found)

    prompt_full, decode_full, gain_full = (
        lax.all_gather(prompt_states, "tensor", axis=1, tiled=True),
        lax.all_gather(decode_states, "tensor", axis=1, tiled=True),
        lax.all_gather(norm_gain[None, :], "tensor", axis=1, tiled=True),
    )
    gain_row = gain_full[0]
    all_normed = normed(jnp.concatenate([decode_full, prompt_full], axis=0), gain_row)
    decode_normed = all_normed[: 2 * DEC]
    row_ids = jnp.arange(D, dtype=jnp.int32)
    query_cols = tensor_id * query_width + jnp.arange(query_width, dtype=jnp.int32)
    pair_cols = tensor_id * pair_width + jnp.arange(pair_width, dtype=jnp.int32)
    tables_left = jnp.concatenate([noise_rows(seed_value, g, row_ids) for g in range(3)], axis=0)
    inner = times_rows(all_normed, tables_left)
    low_query = expand(inner[: 2 * DEC, :RANK], noise_rows(seed_value, 4, query_cols))
    low_key = expand(inner[:, RANK : 2 * RANK], noise_rows(seed_value, 5, pair_cols))
    low_value = expand(inner[:, 2 * RANK :], noise_rows(seed_value, 6, pair_cols))
    low_pair = jnp.concatenate([low_key, low_value], axis=1)
    pair_bias = jnp.concatenate(
        [jnp.zeros((pair_width,), jnp.float32), value_bias.astype(jnp.float32)]
    )
    query_base = jnp.dot(decode_normed, query_all, preferred_element_type=jnp.float32)
    pair_base = jnp.dot(all_normed, pair_all, preferred_element_type=jnp.float32)
    query = (query_base + query_bias.astype(jnp.float32) + column_signs * lift * low_query).astype(
        jnp.bfloat16
    )
    pair_base = pair_base + pair_bias
    mixed_parts = []
    for sign_index in range(2):
        sign = 1.0 - 2.0 * sign_index
        first = sign_index * DEC
        last = first + DEC
        own = jnp.concatenate([pair_base[2 * DEC :], pair_base[first:last]], axis=0)
        own_low = jnp.concatenate([low_pair[2 * DEC :], low_pair[first:last]], axis=0)
        pair = (own + sign * lift * own_low).astype(jnp.bfloat16)
        mixed_parts.append(
            attend(
                query[first:last],
                pair[:, :pair_width],
                pair[:, pair_width:],
                group,
                HEAD_DIM,
                prompt_len,
            )
        )
    mixed = jnp.concatenate(mixed_parts, axis=0)
    out_inner = times_rows(mixed, noise_rows(seed_value, 3, query_cols))
    out_low = expand(out_inner, noise_rows(seed_value, 7, row_ids))
    out_low = column_signs * lift * out_low

    summed = jnp.zeros((2 * DEC, D), jnp.float32)
    for (chip, piece_a), (_, piece_b) in zip(*out_lanes):
        near = jnp.concatenate([piece_a, piece_b], axis=0)
        far = to_sibling(near, members)
        low_part = lax.dynamic_slice_in_dim(out_low, chip * 2 * out_piece, 2 * out_piece, 1)
        partial = []
        for block in (near, far):
            partial.append(times_rows(mixed, block))
        both = [
            jnp.where(core == 0, partial[0], partial[1]),
            jnp.where(core == 0, partial[1], partial[0]),
        ]
        chunk = jnp.concatenate(both, axis=1)
        chunk = (chunk + low_part).astype(jnp.bfloat16)
        if tensors == 2:
            other = lax.ppermute(chunk, "tensor", [(0, 1), (1, 0)])
            chunk = chunk.astype(jnp.float32) + other.astype(jnp.float32)
        else:
            chunk = lax.psum(chunk, "tensor").astype(jnp.float32)
        summed = lax.dynamic_update_slice_in_dim(summed, chunk, chip * 2 * out_piece, 1)

    shared = lax.dynamic_slice_in_dim(summed, tensor_id * shard_width, shard_width, 1)
    difference = shared - targets.astype(jnp.float32)
    fitness_errors = jnp.sum(difference * difference, axis=1) / D
    fitness_errors = jnp.where(row_live, fitness_errors, 0.0)
    pair_total = jnp.stack(
        [
            jnp.sum(fitness_errors[:DEC]) / length_plus.astype(jnp.float32),
            jnp.sum(fitness_errors[DEC:]) / negative_length.astype(jnp.float32),
        ]
    )
    spread = lax.dynamic_update_slice_in_dim(
        jnp.zeros((2 * members,), jnp.float32), pair_total, 2 * member_id, 0
    )
    fitness = -lax.psum(spread, ("member", "tensor"))
    differences = fitness[0::2] - fitness[1::2]
    factor = 1.0 / (2.0 * members * sigma * math.sqrt(RANK))
    row_of_weights = differences * factor
    own_rows = member_id * piece_rows + jnp.arange(piece_rows, dtype=jnp.int32)
    own_out_cols = member_id * out_piece + jnp.arange(out_piece, dtype=jnp.int32)

    def all_rows(matrix_id, ids):
        tables = jax.vmap(lambda seed_one: noise_rows(seed_one, matrix_id, ids))(seeds)
        return tables.reshape(members * RANK, ids.shape[0])

    row_weights = jnp.repeat(row_of_weights, RANK)[:, None]

    def update(first_id, second_id, left_ids, right_ids):
        left = all_rows(first_id, left_ids)
        right = all_rows(second_id, right_ids)
        if left_ids.shape[0] <= right_ids.shape[0]:
            left = jnp.concatenate(parts_of(left.astype(jnp.float32) * row_weights, 2), axis=0)
            right = jnp.concatenate([right, right], axis=0)
        else:
            right = jnp.concatenate(parts_of(right.astype(jnp.float32) * row_weights, 2), axis=0)
            left = jnp.concatenate([left, left], axis=0)
        return lax.dot_general(
            left, right, (((0,), (0,)), ((), ())), preferred_element_type=jnp.float32
        )

    grad_query = update(0, 4, own_rows, query_cols)
    grad_key = update(1, 5, own_rows, pair_cols)
    grad_value = update(2, 6, own_rows, pair_cols)
    grad_out = update(3, 7, query_cols, own_out_cols)
    return (fitness, grad_query, grad_key, grad_value, grad_out)


def solution(mesh):
    placed = (
        P("member", "tensor"),
        P("member", "tensor"),
        P("tensor"),
        P("tensor"),
        P("tensor"),
        P("member", "tensor"),
        P("member", "tensor"),
        P("member", "tensor"),
        P("tensor", "member"),
        P("member", "tensor"),
        P(),
        P(),
    )
    return jax.shard_map(
        per_device,
        mesh=mesh,
        in_specs=placed,
        out_specs=(
            P(),
            P("member", "tensor"),
            P("member", "tensor"),
            P("member", "tensor"),
            P("tensor", "member"),
        ),
        check_vma=False,
    )
```

time: 686 us -> 645 us (0.940); the launches traced: 683 us -> 635 us
  waiting for transfers between devices: 478 us -> 231 us
  local copies, waits for them, and re-layouts: 8.2 us -> 137 us
  other arithmetic: 27.7 us -> 78.1 us
  starting transfers between devices: 0.27 us -> 48.3 us
  matrix products: 108 us -> 61.6 us
  between operations: 18.5 us -> 35.6 us
    all_gather x4 -> x0, waiting for transfers between devices: 311 us -> none  [the longest x1 119 us: per_device(): lax.all_gather(w_query, 'member', axis=0, tiled=True)]
    ppermute x0 -> x64, waiting for transfers between devices: none -> 230 us  [the longest x32 197 us: ring_step(): return lax.ppermute(piece, 'member', perm)]
    dynamic_update_slice x0 -> x72, local copies, waits for them, and re-layouts: none -> 74.1 us  [the longest x32 36.5 us: per_device(): lax.dynamic_update_slice_in_dim(query_all, block[:, :query_width], start, 0)]
    psum x1 -> x0, waiting for transfers between devices: 71.2 us -> none  [per_device(): summed = lax.psum(partial_out, 'tensor').astype(jnp.float32)]
    all_gather x1, waiting for transfers between devices: 66.7 us -> 0.01 us  [per_device(): lax.all_gather(prompt_states, 'tensor', axis=1, tiled=True)]
    ppermute x0 -> x64, starting transfers between devices: none -> 48.3 us  [the longest x32 36.9 us: ring_step(): return lax.ppermute(piece, 'member', perm)]
    dot_general x19 -> x28, matrix products: 101 us -> 54.9 us  [the longest x18 21.3 us: times_rows(): lax.dot_general(left, rows, (((1,), (1,)), ((), ())), preferred_element_t...]
    convert_element_type x2 -> x12, other arithmetic: 3.65 us -> 43.3 us  [the longest x5 26 us: noise_rows(): ((hashed.astype(jnp.float32) * (2.0 / PRIME) - 1.0) * math.sqrt(3.0)).ast...]
  transfers between devices with their start and end apart: 7 -> 66, of which waited for: 7 -> 29; matrix products, arithmetic and copies ran while one was open for 13% -> 39% of each run, Pallas kernels for 0% -> 0%
where the time goes in v1:
time: 645 us; the launch traced here: 635 us
  waiting for transfers between devices  231 us (36%)
  local copies, waits for them, and re-layouts  137 us (21%)
  other arithmetic  78.1 us (12%)
  matrix products  61.6 us (10%)
  starting transfers between devices  48.3 us (7%)
  blocking collectives  43.3 us (7%)
  between operations  35.6 us (6%)
    ppermute x32, waiting for transfers between devices, ring_step(): return lax.ppermute(piece, 'member', perm)  197 us
    psum x1, blocking collectives, per_device(): fitness = -lax.psum(spread, ('member', 'tensor'))  38.7 us
    ppermute x32, starting transfers between devices, ring_step(): return lax.ppermute(piece, 'member', perm)  36.9 us
    dynamic_update_slice x32, local copies, waits for them, and re-layouts, per_device(): lax.dynamic_update_slice_in_dim(query_all, block[:, :query_width], start, 0)  36.5 us
    ppermute x8, waiting for transfers between devices, per_device(): other = lax.ppermute(chunk, 'tensor', [(0, 1), (1, 0)])  33.2 us
    dynamic_update_slice x32, local copies, waits for them, and re-layouts, per_device(): lax.dynamic_update_slice_in_dim(pair_all, block[:, query_width:], start, 0)  29.2 us
    convert_element_type x5, other arithmetic, noise_rows(): ((hashed.astype(jnp.float32) * (2.0 / PRIME) - 1.0) * math.sqrt(3.0)).ast...  26 us
    dot_general x18, matrix products, times_rows(): lax.dot_general(left, rows, (((1,), (1,)), ((), ())), preferred_element_t...  21.3 us
  transfers between devices with their start and end apart: 66, of which 29 were waited for; matrix products, arithmetic and copies ran while one was open for 39% of the time, Pallas kernels for 0%

profile of v1, /device:TPU:0, one launch (start us, length us, event | category | flops | bytes accessed | tf_op | source)
XLA Modules:
  0.0 635.0 jit_solution(197079758639194925)
XLA Ops:
  38.8 8.9 %broadcast_in_dim.51 = bf16[5120,2560]{1,0:T(8,128)(2,1)} broadcast(bf16[]{:T(256)} %constant.470.clone.1), dimensions={} | broadcast | bytes 26214402 | tf_op jit(solution)/shard_map/broadcast_in_dim | solution.py:174
  55.8 15.6 %fusion.44 = (bf16[256,2560]{1,0:T(8,128)(2,1)}, bf16[256,2560]{1,0:T(8,128)(2,1)}) fusion(s32[256]{0:T(256)S(1)} %get-tuple-element.90, s32[2560]{0:T(1024)S(1)} %add_multiply_fusion, s32[256]{0:T(256)S(1)} %get-tuple-element.95), kind=kLoop, calls=%fused_computation.72 | loop fusion | flops 47185920 | bytes 2633728 | tf_op jit(solution)/shard_map/vmap()/convert_element_type | solution.py:29
  106.2 16.2 %collective-permute-done.5 = bf16[160,3584]{1,0:T(8,128)(2,1)S(1)} collective-permute-done((bf16[160,3584]{1,0:T(8,128)(2,1)}, bf16[160,3584]{1,0:T(8,128)(2,1)S(1)}, u32[]{:S(2)}, u32[]{:S(2)}) %collective-permute-start.5) | collective-permute-done | bytes 1146912 | tf_op jit(solution)/shard_map/ppermute | solution.py:101
  132.4 14.5 %collective-permute-done.21 = bf16[160,3584]{1,0:T(8,128)(2,1)S(1)} collective-permute-done((bf16[160,3584]{1,0:T(8,128)(2,1)}, bf16[160,3584]{1,0:T(8,128)(2,1)S(1)}, u32[]{:S(2)}, u32[]{:S(2)}) %collective-permute-start.21) | collective-permute-done | bytes 1146912 | tf_op jit(solution)/shard_map/ppermute | solution.py:101
  148.9 7.8 %collective-permute-done.23 = bf16[160,3584]{1,0:T(8,128)(2,1)S(1)} collective-permute-done((bf16[160,3584]{1,0:T(8,128)(2,1)}, bf16[160,3584]{1,0:T(8,128)(2,1)S(1)}, u32[]{:S(2)}, u32[]{:S(2)}) %collective-permute-start.23) | collective-permute-done | bytes 1146912 | tf_op jit(solution)/shard_map/ppermute | solution.py:101
  161.4 10.1 %collective-permute-done.9 = bf16[160,3584]{1,0:T(8,128)(2,1)S(1)} collective-permute-done((bf16[160,3584]{1,0:T(8,128)(2,1)S(1)}, bf16[160,3584]{1,0:T(8,128)(2,1)S(1)}, u32[]{:S(2)}, u32[]{:S(2)}) %collective-permute-start.9) | collective-permute-done | bytes 1146912 | tf_op jit(solution)/shard_map/ppermute | solution.py:101
  171.6 9.8 %collective-permute-done.11 = bf16[160,3584]{1,0:T(8,128)(2,1)S(1)} collective-permute-done((bf16[160,3584]{1,0:T(8,128)(2,1)S(1)}, bf16[160,3584]{1,0:T(8,128)(2,1)S(1)}, u32[]{:S(2)}, u32[]{:S(2)}) %collective-permute-start.11) | collective-permute-done | bytes 1146912 | tf_op jit(solution)/shard_map/ppermute | solution.py:101
  182.9 13.2 %collective-permute-done.25 = bf16[160,3584]{1,0:T(8,128)(2,1)S(1)} collective-permute-done((bf16[160,3584]{1,0:T(8,128)(2,1)S(1)}, bf16[160,3584]{1,0:T(8,128)(2,1)S(1)}, u32[]{:S(2)}, u32[]{:S(2)}) %collective-permute-start.25) | collective-permute-done | bytes 1146912 | tf_op jit(solution)/shard_map/ppermute | solution.py:101
  198.0 7.9 %collective-permute-done.27 = bf16[160,3584]{1,0:T(8,128)(2,1)S(1)} collective-permute-done((bf16[160,3584]{1,0:T(8,128)(2,1)S(1)}, bf16[160,3584]{1,0:T(8,128)(2,1)S(1)}, u32[]{:S(2)}, u32[]{:S(2)}) %collective-permute-start.27) | collective-permute-done | bytes 1146912 | tf_op jit(solution)/shard_map/ppermute | solution.py:101
  222.1 8.4 %collective-permute-done.30 = bf16[80,3584]{1,0:T(8,128)(2,1)S(1)} collective-permute-done((bf16[80,3584]{1,0:T(8,128)(2,1)S(1)}, bf16[80,3584]{1,0:T(8,128)(2,1)S(1)}, u32[]{:S(2)}, u32[]{:S(2)}) %collective-permute-start.30) | collective-permute-done | bytes 573472 | tf_op jit(solution)/shard_map/ppermute | solution.py:101
  240.7 7.4 %collective-permute-done.38 = bf16[160,2560]{1,0:T(8,128)(2,1)S(1)} collective-permute-done((bf16[160,2560]{1,0:T(8,128)(2,1)S(1)}, bf16[160,2560]{1,0:T(8,128)(2,1)S(1)}, u32[]{:S(2)}, u32[]{:S(2)}) %collective-permute-start.38) | collective-permute-done | bytes 819232 | tf_op jit(solution)/shard_map/ppermute | solution.py:101
  254.1 10.9 %collective-permute-done.39 = bf16[160,2560]{1,0:T(8,128)(2,1)S(1)} collective-permute-done((bf16[160,2560]{1,0:T(8,128)(2,1)S(1)}, bf16[160,2560]{1,0:T(8,128)(2,1)S(1)}, u32[]{:S(2)}, u32[]{:S(2)}) %collective-permute-start.39) | collective-permute-done | bytes 819232 | tf_op jit(solution)/shard_map/ppermute | solution.py:101
  322.1 11.0 %convolution_add_fusion.1 = f32[768,1024]{1,0:T(8,128)S(1)} fusion(bf16[768,5120]{1,0:T(8,128)(2,1)S(1)} %fusion.4, bf16[5120,1024]{1,0:T(8,128)(2,1)} %slice_dynamic-update-slice_fusion.32, f32[1024]{0:T(1024)S(1)} %copy-done.35), kind=kOutput, calls=%fused_computation.102 | convolution fusion | flops 8053850112 | bytes 21499904 | tf_op jit(solution)/shard_map/dot_general | solution.py:213
  342.1 12.5 %fusion.8 = bf16[256,2560]{1,0:T(8,128)(2,1)S(1)} fusion(f32[256,2560]{1,0:T(8,128)S(1)} %convolution_multiply_fusion.1, bf16[5120,2560]{1,0:T(8,128)(2,1)} %slice_dynamic-update-slice_fusion, bf16[768,5120]{1,0:T(8,128)(2,1)S(1)} %fusion.4, f32[2560]{0:T(1024)S(1)} %copy-done.31), kind=kOutput, calls=%fused_computation.28 | convolution fusion | flops 6712852480 | bytes 32780288 | tf_op jit(solution)/shard_map/dot_general | solution.py:212
  365.8 10.1 %reshape.484 = bf16[640,4,128]{2,1,0:T(4,128)(2,1)S(1)} reshape(bf16[640,512]{1,0:T(8,128)(2,1)} %get-tuple-element.31) | data formatting | bytes 1310720 | tf_op jit(solution)/shard_map/reshape | solution.py:68
  400.3 16.1 %collective-permute-done.46 = bf16[160,2560]{1,0:T(8,128)(2,1)S(1)} collective-permute-done((bf16[160,2560]{1,0:T(8,128)(2,1)S(1)}, bf16[160,2560]{1,0:T(8,128)(2,1)S(1)}, u32[]{:S(2)}, u32[]{:S(2)}) %collective-permute-start.46) | collective-permute-done | bytes 819232 | tf_op jit(solution)/shard_map/ppermute | solution.py:101
  418.0 14.4 %collective-permute-done.47 = bf16[160,2560]{1,0:T(8,128)(2,1)S(1)} collective-permute-done((bf16[160,2560]{1,0:T(8,128)(2,1)S(1)}, bf16[160,2560]{1,0:T(8,128)(2,1)S(1)}, u32[]{:S(2)}, u32[]{:S(2)}) %collective-permute-start.47) | collective-permute-done | bytes 819232 | tf_op jit(solution)/shard_map/ppermute | solution.py:101
  440.7 10.7 %collective-permute-done.50 = bf16[160,2560]{1,0:T(8,128)(2,1)S(1)} collective-permute-done((bf16[160,2560]{1,0:T(8,128)(2,1)}, bf16[160,2560]{1,0:T(8,128)(2,1)S(1)}, u32[]{:S(2)}, u32[]{:S(2)}) %collective-permute-start.50) | collective-permute-done | bytes 819232 | tf_op jit(solution)/shard_map/ppermute | solution.py:101
  452.1 20.2 %collective-permute-done.54 = bf16[160,2560]{1,0:T(8,128)(2,1)S(1)} collective-permute-done((bf16[160,2560]{1,0:T(8,128)(2,1)S(1)}, bf16[160,2560]{1,0:T(8,128)(2,1)S(1)}, u32[]{:S(2)}, u32[]{:S(2)}) %collective-permute-start.54) | collective-permute-done | bytes 819232 | tf_op jit(solution)/shard_map/ppermute | solution.py:101
  486.3 8.6 %collective-permute-done.59 = bf16[80,2560]{1,0:T(8,128)(2,1)S(1)} collective-permute-done((bf16[80,2560]{1,0:T(8,128)(2,1)S(1)}, bf16[80,2560]{1,0:T(8,128)(2,1)S(1)}, u32[]{:S(2)}, u32[]{:S(2)}) %collective-permute-start.59) | collective-permute-done | bytes 409632 | tf_op jit(solution)/shard_map/ppermute | solution.py:101
  495.6 9.1 %collective-permute-done.61 = bf16[80,2560]{1,0:T(8,128)(2,1)S(1)} collective-permute-done((bf16[80,2560]{1,0:T(8,128)(2,1)S(1)}, bf16[80,2560]{1,0:T(8,128)(2,1)S(1)}, u32[]{:S(2)}, u32[]{:S(2)}) %collective-permute-start.61) | collective-permute-done | bytes 409632 | tf_op jit(solution)/shard_map/ppermute | solution.py:101
  531.5 6.9 %collective-permute-done.53 = bf16[256,640]{0,1:T(8,128)(2,1)S(1)} collective-permute-done((bf16[256,640]{0,1:T(8,128)(2,1)S(1)}, bf16[256,640]{0,1:T(8,128)(2,1)S(1)}, u32[]{:S(2)}, u32[]{:S(2)}) %collective-permute-start.53) | collective-permute-done | bytes 327712 | tf_op jit(solution)/shard_map/ppermute | solution.py:256
  538.5 6.9 %collective-permute-done.49 = bf16[256,640]{0,1:T(8,128)(2,1)S(1)} collective-permute-done((bf16[256,640]{0,1:T(8,128)(2,1)S(1)}, bf16[256,640]{0,1:T(8,128)(2,1)S(1)}, u32[]{:S(2)}, u32[]{:S(2)}) %collective-permute-start.49) | collective-permute-done | bytes 327712 | tf_op jit(solution)/shard_map/ppermute | solution.py:256
  575.7 38.7 %psum.7 = f32[32]{0:T(128)S(1)} all-reduce(f32[32]{0:T(128)S(1)} %maximum_dynamic-update-slice_fusion), channel_id=1, replica_groups=mesh['member'=16,'tensor'=2] {'member','tensor'}, use_global_device_ids=true, to_apply=%region_8.9 | all-reduce | flops 32 | bytes 256 | tf_op jit(solution)/shard_map/psum | solution.py:275
  (446 shorter events, 303.7 us)
Async XLA Ops:
  7.2 302.5 %all-gather.5.cloned.1.call-start = ((), (), s32[]{:S(2)}) async-start(), calls=%async_computation | async-start | bytes 3932160 | tf_op jit(solution)/shard_map/all_gather | solution.py:194
  7.9 301.8 %all-gather.7.cloned.1.call-start = ((), (), s32[]{:S(2)}) async-start(), calls=%async_computation.1 | async-start | bytes 7864320 | tf_op jit(solution)/shard_map/all_gather | solution.py:193
  12.0 81.9 %collective-permute-start = (bf16[160,3584]{1,0:T(8,128)(2,1)}, bf16[160,3584]{1,0:T(8,128)(2,1)}, u32[]{:S(2)}, u32[]{:S(2)}) collective-permute-start(bf16[160,3584]{1,0:T(8,128)(2,1)} %get-tuple-element.24), channel_id=1, source_target_pairs={{0,2},{2,0},{4,6},{6,4},{8,10},{10,8},{12,14},{14,12},{16,18},{18,... | collective-permute-start | bytes 3440648 | tf_op jit(solution)/shard_map/ppermute | solution.py:105
  12.5 81.4 %collective-permute-start.1 = (bf16[160,3584]{1,0:T(8,128)(2,1)}, bf16[160,3584]{1,0:T(8,128)(2,1)}, u32[]{:S(2)}, u32[]{:S(2)}) collective-permute-start(bf16[160,3584]{1,0:T(8,128)(2,1)} %get-tuple-element.24), channel_id=1, source_target_pairs={{0,8},{2,10},{8,16},{10,18},{16,24},{18,26},{24,28},{26,30},{28,20... | collective-permute-start | bytes 3440648 | tf_op jit(solution)/shard_map/ppermute | solution.py:101
  15.1 81.0 %collective-permute-start.3 = (bf16[160,3584]{1,0:T(8,128)(2,1)}, bf16[160,3584]{1,0:T(8,128)(2,1)}, u32[]{:S(2)}, u32[]{:S(2)}) collective-permute-start(bf16[160,3584]{1,0:T(8,128)(2,1)} %get-tuple-element.24), channel_id=1, source_target_pairs={{0,4},{2,6},{8,0},{10,2},{16,8},{18,10},{24,16},{26,18},{28,24},{3... | collective-permute-start | bytes 3440648 | tf_op jit(solution)/shard_map/ppermute | solution.py:101
  15.1 88.7 %collective-permute-start.17 = (bf16[160,3584]{1,0:T(8,128)(2,1)}, bf16[160,3584]{1,0:T(8,128)(2,1)}, u32[]{:S(2)}, u32[]{:S(2)}) collective-permute-start(bf16[160,3584]{1,0:T(8,128)(2,1)} %get-tuple-element.23), channel_id=1, source_target_pairs={{0,8},{2,10},{8,16},{10,18},{16,24},{18,26},{24,28},{26,30},{28,20... | collective-permute-start | bytes 3440648 | tf_op jit(solution)/shard_map/ppermute | solution.py:101
  17.1 87.0 %collective-permute-start.19 = (bf16[160,3584]{1,0:T(8,128)(2,1)}, bf16[160,3584]{1,0:T(8,128)(2,1)}, u32[]{:S(2)}, u32[]{:S(2)}) collective-permute-start(bf16[160,3584]{1,0:T(8,128)(2,1)} %get-tuple-element.23), channel_id=1, source_target_pairs={{0,4},{2,6},{8,0},{10,2},{16,8},{18,10},{24,16},{26,18},{28,24},{3... | collective-permute-start | bytes 3440648 | tf_op jit(solution)/shard_map/ppermute | solution.py:101
  104.2 42.8 %collective-permute-start.21 = (bf16[160,3584]{1,0:T(8,128)(2,1)}, bf16[160,3584]{1,0:T(8,128)(2,1)S(1)}, u32[]{:S(2)}, u32[]{:S(2)}) collective-permute-start(bf16[160,3584]{1,0:T(8,128)(2,1)} %collective-permute-done.17), channel_id=1, source_target_pairs={{0,8},{2,10},{8,16},{10,18},{16,24},{18,26},{24,28},{26,30},{28,20... | collective-permute-start | bytes 3440648 | tf_op jit(solution)/shard_map/ppermute | solution.py:101
  105.9 50.8 %collective-permute-start.23 = (bf16[160,3584]{1,0:T(8,128)(2,1)}, bf16[160,3584]{1,0:T(8,128)(2,1)S(1)}, u32[]{:S(2)}, u32[]{:S(2)}) collective-permute-start(bf16[160,3584]{1,0:T(8,128)(2,1)} %collective-permute-done.19), channel_id=1, source_target_pairs={{0,4},{2,6},{8,0},{10,2},{16,8},{18,10},{24,16},{26,18},{28,24},{3... | collective-permute-start | bytes 3440648 | tf_op jit(solution)/shard_map/ppermute | solution.py:101
  122.4 38.1 %collective-permute-start.6 = (bf16[160,3584]{1,0:T(8,128)(2,1)S(1)}, bf16[160,3584]{1,0:T(8,128)(2,1)S(1)}, u32[]{:S(2)}, u32[]{:S(2)}) collective-permute-start(bf16[160,3584]{1,0:T(8,128)(2,1)S(1)} %collective-permute-done.5), channel_id=1, source_target_pairs={{0,2},{2,0},{4,6},{6,4},{8,10},{10,8},{12,14},{14,12},{16,18},{18,... | collective-permute-start | bytes 3440648 | tf_op jit(solution)/shard_map/ppermute | solution.py:105
  128.0 43.5 %collective-permute-start.9 = (bf16[160,3584]{1,0:T(8,128)(2,1)S(1)}, bf16[160,3584]{1,0:T(8,128)(2,1)S(1)}, u32[]{:S(2)}, u32[]{:S(2)}) collective-permute-start(bf16[160,3584]{1,0:T(8,128)(2,1)S(1)} %collective-permute-done.5), channel_id=1, source_target_pairs={{0,8},{2,10},{8,16},{10,18},{16,24},{18,26},{24,28},{26,30},{28,20... | collective-permute-start | bytes 3440648 | tf_op jit(solution)/shard_map/ppermute | solution.py:101
  132.2 49.2 %collective-permute-start.11 = (bf16[160,3584]{1,0:T(8,128)(2,1)S(1)}, bf16[160,3584]{1,0:T(8,128)(2,1)S(1)}, u32[]{:S(2)}, u32[]{:S(2)}) collective-permute-start(bf16[160,3584]{1,0:T(8,128)(2,1)S(1)} %collective-permute-done.7), channel_id=1, source_target_pairs={{0,4},{2,6},{8,0},{10,2},{16,8},{18,10},{24,16},{26,18},{28,24},{3... | collective-permute-start | bytes 3440648 | tf_op jit(solution)/shard_map/ppermute | solution.py:101
  146.9 49.2 %collective-permute-start.25 = (bf16[160,3584]{1,0:T(8,128)(2,1)S(1)}, bf16[160,3584]{1,0:T(8,128)(2,1)S(1)}, u32[]{:S(2)}, u32[]{:S(2)}) collective-permute-start(bf16[160,3584]{1,0:T(8,128)(2,1)S(1)} %collective-permute-done.21), channel_id=1, source_target_pairs={{0,8},{2,10},{8,16},{10,18},{16,24},{18,26},{24,28},{26,30},{28,20... | collective-permute-start | bytes 3440648 | tf_op jit(solution)/shard_map/ppermute | solution.py:101
  156.8 49.2 %collective-permute-start.27 = (bf16[160,3584]{1,0:T(8,128)(2,1)S(1)}, bf16[160,3584]{1,0:T(8,128)(2,1)S(1)}, u32[]{:S(2)}, u32[]{:S(2)}) collective-permute-start(bf16[160,3584]{1,0:T(8,128)(2,1)S(1)} %collective-permute-done.23), channel_id=1, source_target_pairs={{0,4},{2,6},{8,0},{10,2},{16,8},{18,10},{24,16},{26,18},{28,24},{3... | collective-permute-start | bytes 3440648 | tf_op jit(solution)/shard_map/ppermute | solution.py:101
  160.4 48.7 %collective-permute-start.8 = (bf16[160,3584]{1,0:T(8,128)(2,1)S(1)}, bf16[160,3584]{1,0:T(8,128)(2,1)S(1)}, u32[]{:S(2)}, u32[]{:S(2)}) collective-permute-start(bf16[160,3584]{1,0:T(8,128)(2,1)S(1)} %collective-permute-done.7), channel_id=1, source_target_pairs={{0,2},{2,0},{4,6},{6,4},{8,10},{10,8},{12,14},{14,12},{16,18},{18,... | collective-permute-start | bytes 3440648 | tf_op jit(solution)/shard_map/ppermute | solution.py:105
  171.5 103.0 %collective-permute-start.16 = (bf16[160,3584]{1,0:T(8,128)(2,1)}, bf16[160,3584]{1,0:T(8,128)(2,1)S(1)}, u32[]{:S(2)}, u32[]{:S(2)}) collective-permute-start(bf16[160,3584]{1,0:T(8,128)(2,1)} %get-tuple-element.23), channel_id=1, source_target_pairs={{0,2},{2,0},{4,6},{6,4},{8,10},{10,8},{12,14},{14,12},{16,18},{18,... | collective-permute-start | bytes 3440648 | tf_op jit(solution)/shard_map/ppermute | solution.py:105
  287.8 110.4 %collective-permute-start.32 = (bf16[320,2560]{1,0:T(8,128)(2,1)}, bf16[320,2560]{1,0:T(8,128)(2,1)}, u32[]{:S(2)}, u32[]{:S(2)}) collective-permute-start(bf16[320,2560]{1,0:T(8,128)(2,1)} %constant_dynamic-update-slice_fusion.3), channel_id=1, source_target_pairs={{0,2},{2,0},{4,6},{6,4},{8,10},{10,8},{12,14},{14,12},{16,18},{18,... | collective-permute-start | bytes 4915208 | tf_op jit(solution)/shard_map/ppermute | solution.py:105
  290.7 183.5 %collective-permute-start.40 = (bf16[320,2560]{1,0:T(8,128)(2,1)}, bf16[320,2560]{1,0:T(8,128)(2,1)}, u32[]{:S(2)}, u32[]{:S(2)}) collective-permute-start(bf16[320,2560]{1,0:T(8,128)(2,1)} %constant_dynamic-update-slice_fusion.13), channel_id=1, source_target_pairs={{0,2},{2,0},{4,6},{6,4},{8,10},{10,8},{12,14},{14,12},{16,18},{18,... | collective-permute-start | bytes 4915208 | tf_op jit(solution)/shard_map/ppermute | solution.py:105
  293.3 142.8 %collective-permute-start.36 = (bf16[320,2560]{1,0:T(8,128)(2,1)}, bf16[320,2560]{1,0:T(8,128)(2,1)}, u32[]{:S(2)}, u32[]{:S(2)}) collective-permute-start(bf16[320,2560]{1,0:T(8,128)(2,1)} %constant_dynamic-update-slice_fusion.11), channel_id=1, source_target_pairs={{0,2},{2,0},{4,6},{6,4},{8,10},{10,8},{12,14},{14,12},{16,18},{18,... | collective-permute-start | bytes 4915208 | tf_op jit(solution)/shard_map/ppermute | solution.py:105
  296.1 100.7 %collective-permute-start.43 = (bf16[160,2560]{1,0:T(8,128)(2,1)}, bf16[160,2560]{1,0:T(8,128)(2,1)}, u32[]{:S(2)}, u32[]{:S(2)}) collective-permute-start(bf16[160,2560]{1,0:T(8,128)(2,1)} %collective-permute-done.35), channel_id=1, source_target_pairs={{0,8},{2,10},{8,16},{10,18},{16,24},{18,26},{24,28},{26,30},{28,20... | collective-permute-start | bytes 2457608 | tf_op jit(solution)/shard_map/ppermute | solution.py:101
  300.4 94.6 %collective-permute-start.42 = (bf16[160,2560]{1,0:T(8,128)(2,1)}, bf16[160,2560]{1,0:T(8,128)(2,1)}, u32[]{:S(2)}, u32[]{:S(2)}) collective-permute-start(bf16[160,2560]{1,0:T(8,128)(2,1)} %collective-permute-done.34), channel_id=1, source_target_pairs={{0,8},{2,10},{8,16},{10,18},{16,24},{18,26},{24,28},{26,30},{28,20... | collective-permute-start | bytes 2457608 | tf_op jit(solution)/shard_map/ppermute | solution.py:101
  398.2 108.0 %collective-permute-start.44 = (bf16[320,2560]{1,0:T(8,128)(2,1)S(1)}, bf16[320,2560]{1,0:T(8,128)(2,1)S(1)}, u32[]{:S(2)}, u32[]{:S(2)}) collective-permute-start(bf16[320,2560]{1,0:T(8,128)(2,1)S(1)} %constant_dynamic-update-slice_fusion.15), channel_id=1, source_target_pairs={{0,2},{2,0},{4,6},{6,4},{8,10},{10,8},{12,14},{14,12},{16,18},{18,... | collective-permute-start | bytes 4915208 | tf_op jit(solution)/shard_map/ppermute | solution.py:105
  452.0 55.6 %collective-permute-start.48 = (bf16[320,2560]{1,0:T(8,128)(2,1)S(1)}, bf16[320,2560]{1,0:T(8,128)(2,1)S(1)}, u32[]{:S(2)}, u32[]{:S(2)}) collective-permute-start(bf16[320,2560]{1,0:T(8,128)(2,1)S(1)} %constant_dynamic-update-slice_fusion.17), channel_id=1, source_target_pairs={{0,2},{2,0},{4,6},{6,4},{8,10},{10,8},{12,14},{14,12},{16,18},{18,... | collective-permute-start | bytes 4915208 | tf_op jit(solution)/shard_map/ppermute | solution.py:105
  472.3 36.5 %collective-permute-start.52 = (bf16[320,2560]{1,0:T(8,128)(2,1)S(1)}, bf16[320,2560]{1,0:T(8,128)(2,1)S(1)}, u32[]{:S(2)}, u32[]{:S(2)}) collective-permute-start(bf16[320,2560]{1,0:T(8,128)(2,1)S(1)} %constant_dynamic-update-slice_fusion.19), channel_id=1, source_target_pairs={{0,2},{2,0},{4,6},{6,4},{8,10},{10,8},{12,14},{14,12},{16,18},{18,... | collective-permute-start | bytes 4915208 | tf_op jit(solution)/shard_map/ppermute | solution.py:105
  (89 other events, 1481.4 us)
Sparse Core Ops, SparseCore 0:
  9.6 41.7 all-gather.4
  52.9 68.7 all-gather.6
